TPU v7x, 32 devices: a whole 2x2x4 slice. The times are simulated.
32 devices in a mesh: rep: 2 (over x), tp: 16 (over z, y, core).
Axes of the slice: x: 2, y: 2, z: 4, core: 2. Of those that a mesh axis runs over, the one named last changes fastest.
Arguments:
- layer_input: bfloat16 [256, 8192], P(('rep', 'tp')), parts along dimension 0, may hold values from -400 to 400
- input_norm_gain: float32 [8192], replicated, may hold values from 0.5 to 2
- query_weight: bfloat16 [8192, 8192], P(None, 'tp'), may hold values from -1 to 1
- key_value_weight: bfloat16 [8192, 2048], P(None, 'tp'), may hold values from -1 to 1
- output_weight: bfloat16 [8192, 8192], P('tp'), may hold values from -0.125 to 0.125
- cached_key_value: bfloat16 [2, 4, 65536, 128], P(None, 'rep', 'tp'), parts along dimension 1, may hold values from -300 to 300
- adapter_down_weight: bfloat16 [32, 48, 8192], P('tp'), may hold values from -0.0625 to 0.0625
- adapter_up_weight: bfloat16 [32, 16, 10240], P('tp'), may hold values from -1.5 to 1.5
- request_adapter: int32 [4], P('rep'), parts along dimension 0, may hold values from 0 to 31
- adapter_storage_index: int32 [32], replicated, may hold values from 0 to 31, each once
- cached_length: int32 [4], P('rep'), parts along dimension 0, may hold values from 2048 to 8192, as said below
- parent_node: int32 [4, 64], P('rep'), parts along dimension 0, may hold values from 0 to 62, as said below
Outputs:
- attn_out: bfloat16 [256, 8192], P(('rep', 'tp')), parts along dimension 0
There are 2 independent parts, one for each index of `rep`. A program takes and returns all parts, laid end to end along the dimension named above; an argument that names none is the same for every part. Nothing has to cross between parts.
Inputs may be any that keep to these rules, and one draw needn't show every extreme that they name: `cached_length`: at least one request has exactly 8192 cached tokens. parent_node[r, 0] = 0 marks the root; every other node i has a parent from i - 8 to i - 1, and the last node's parent is the node just before it.
All inputs are finite; a program needn't handle non-finite values.
Results may differ from a plain program's by a relative error of at most 0.015.
The roundings to bfloat16 on the way count: a program that leaves them out, or rounds other values in their place, can miss the bound.
Values may be sent and summed in bfloat16 or wider, within the bound.
A program may use at most 128 MiB of HBM per device.

v0:
```python
import math

import jax
import jax.numpy as jnp
from jax import lax
from jax.sharding import PartitionSpec as P

KEY_HEADS = 8


epsilon = 1e-05
adapter_scale = 0.5
rope_base = 500000.0
masked_score = -1e30


def broadcast(block, axis, source):
    block = jnp.where(lax.axis_index(axis) == source, block, jnp.zeros_like(block))
    return lax.psum(block, axis)


def partner_2(value, axis, stride):
    mask = 2**stride
    pairs = [(source, source ^ mask) for source in range(lax.axis_size(axis))]
    return lax.ppermute(value, axis, pairs)


def for_sending(x):

    def short(part):
        return part.astype(jnp.bfloat16) if part.dtype == jnp.float32 else part

    return jax.tree.map(short, x)


def normalize(hidden_rows, input_norm_gain):
    widened = hidden_rows.astype(jnp.float32)
    squares_mean = jnp.mean(widened * widened, axis=-1, keepdims=True)
    return (widened * lax.rsqrt(squares_mean + epsilon) * input_norm_gain).astype(jnp.bfloat16)


def ancestors(parents):
    node_count = parents.shape[0]
    node_index = jnp.arange(node_count, dtype=jnp.int32)
    parent_hot = (parents[:, None] == node_index[None, :]).astype(jnp.float32)
    reached = jnp.maximum(parent_hot, jnp.eye(node_count, dtype=jnp.float32))
    for repeat in range(node_count.bit_length()):
        reached = jnp.minimum(jnp.dot(reached, reached, precision=lax.Precision.HIGHEST), 1.0)
    return reached


def rotate(vectors, positions):
    half_dim = vectors.shape[-1] // 2
    exponents = jnp.arange(half_dim, dtype=jnp.float32) * (2.0 / vectors.shape[-1])
    inverse = jnp.exp(exponents * -math.log(rope_base))
    angles = positions.astype(jnp.float32)[:, None, None] * inverse[None, None, :]
    cosine = jnp.cos(angles)
    sine_part = jnp.sin(angles)
    leading = vectors[..., :half_dim]
    second = vectors[..., half_dim:]
    return jnp.concatenate(
        [leading * cosine - second * sine_part, second * cosine + leading * sine_part], axis=-1
    )


def project_down(tree_token_rows, down_result):
    return lax.dot_general(
        tree_token_rows, down_result, (((1,), (1,)), ((), ())), preferred_element_type=jnp.float32
    ).astype(jnp.bfloat16)


def spread(per_head, offset, width, head_dim):
    expanded = jnp.repeat(per_head, head_dim, axis=1)
    return lax.dynamic_slice_in_dim(expanded, offset, width, 1)


def combine(own_state, other_state, offset, head_dim):
    width = own_state[0].shape[1]
    new_top = jnp.maximum(own_state[1], other_state[1])
    own_factor = jnp.exp(own_state[1] - new_top)
    other_factor = jnp.exp(other_state[1] - new_top)
    new_total = own_state[2] * own_factor + other_state[2] * other_factor
    new_values = own_state[0] * spread(own_factor, offset, width, head_dim) + other_state[
        0
    ] * spread(other_factor, offset, width, head_dim)
    return (new_values, new_top, new_total)


def partial_attention(queries, all_keys, all_values, usable, group_heads):
    scores = lax.dot_general(
        queries, all_keys, (((1,), (1,)), ((), ())), preferred_element_type=jnp.float32
    ) * all_keys.shape[1] ** (-0.5)
    mask_rows = jnp.repeat(usable, group_heads, axis=0)
    scores = jnp.where(mask_rows, scores, masked_score)
    row_top = jnp.max(scores, axis=1, keepdims=True)
    weights = jnp.where(mask_rows, jnp.exp(scores - row_top), 0.0)
    row_total = jnp.sum(weights, axis=1, keepdims=True)
    blended = jnp.dot(weights.astype(jnp.bfloat16), all_values, preferred_element_type=jnp.float32)
    return (blended, row_top, row_total)


def body(
    layer_input,
    input_norm_gain,
    query_weight,
    key_value_weight,
    output_weight,
    cached_key_value,
    adapter_down_weight,
    adapter_up_weight,
    request_adapter,
    adapter_storage_index,
    cached_length,
    parent_node,
):
    devices = lax.axis_size("tp")
    device = lax.axis_index("tp")
    model_dim = query_weight.shape[0]
    query_cols = query_weight.shape[1]
    pair_cols = key_value_weight.shape[1]
    storage_slot_list = adapter_down_weight.shape[0]
    total_rank = adapter_down_weight.shape[1]
    rank_size = total_rank // 3
    requests = request_adapter.shape[0]
    tree_size = parent_node.shape[1]
    head_dim = cached_key_value.shape[3]
    block_keys = cached_key_value.shape[2]
    kv_width = pair_cols * devices // 2
    group_size = devices // KEY_HEADS
    depth_levels = group_size.bit_length() - 1
    head_group = device // group_size
    member = device % group_size
    group_width = query_cols * group_size
    group_heads = group_width // head_dim
    tree_block = tree_size // group_size
    everyone = lax.all_gather(layer_input, "tp", axis=0, tiled=True)
    normed = normalize(everyone, input_norm_gain)
    kv_start = device * pair_cols
    is_value = kv_start >= kv_width
    query_blocks = []
    pair_blocks = []
    for request in range(requests):
        storage_slot_index = adapter_storage_index[request_adapter[request]]
        owner_index = storage_slot_index // storage_slot_list
        slot_local = storage_slot_index % storage_slot_list
        request_down = lax.dynamic_index_in_dim(adapter_down_weight, slot_local, 0, keepdims=False)
        request_up = lax.dynamic_index_in_dim(adapter_up_weight, slot_local, 0, keepdims=False)
        tree_token_rows = normed[request * tree_size : (request + 1) * tree_size]
        down_result, up_result = (
            broadcast(request_down, "tp", owner_index),
            broadcast(request_up, "tp", owner_index),
        )
        low_rank = project_down(tree_token_rows, down_result)
        query_update = jnp.dot(
            low_rank[:, :rank_size],
            lax.dynamic_slice_in_dim(up_result, device * query_cols, query_cols, 1),
            preferred_element_type=jnp.float32,
        )
        query_blocks.append(
            (
                jnp.dot(tree_token_rows, query_weight, preferred_element_type=jnp.float32)
                + adapter_scale * query_update
            ).astype(jnp.bfloat16)
        )
        pair_rank = jnp.where(
            is_value, low_rank[:, 2 * rank_size :], low_rank[:, rank_size : 2 * rank_size]
        )
        paired_update = jnp.dot(
            pair_rank,
            lax.dynamic_slice_in_dim(up_result, model_dim + kv_start, pair_cols, 1),
            preferred_element_type=jnp.float32,
        )
        pair_blocks.append(
            (
                jnp.dot(tree_token_rows, key_value_weight, preferred_element_type=jnp.float32)
                + adapter_scale * paired_update
            ).astype(jnp.bfloat16)
        )
    query_local = jnp.concatenate(query_blocks, axis=0)
    pair_local = jnp.concatenate(pair_blocks, axis=0)
    pair_all = lax.all_gather(pair_local, "tp", axis=1, tiled=True)
    query_group = query_local
    for section_bit in range(depth_levels):
        partner = partner_2(query_group, "tp", section_bit)
        upper_half = member // 2**section_bit % 2 == 1
        query_group = jnp.concatenate(
            [
                jnp.where(upper_half, partner, query_group),
                jnp.where(upper_half, query_group, partner),
            ],
            axis=1,
        )
    key_cols = lax.dynamic_slice_in_dim(pair_all, head_group * head_dim, head_dim, 1)
    value_cols = lax.dynamic_slice_in_dim(pair_all, kv_width + head_group * head_dim, head_dim, 1)
    block_index = member * block_keys + jnp.arange(block_keys, dtype=jnp.int32)
    value_parts = []
    top_parts = []
    total_parts = []
    for request in range(requests):
        reached = ancestors(parent_node[request])
        node_depth = jnp.sum(reached, axis=1).astype(jnp.int32) - 1
        positions = cached_length[request] + node_depth
        request_queries = query_group[request * tree_size : (request + 1) * tree_size]
        queries = (
            rotate(
                request_queries.astype(jnp.float32).reshape(tree_size, group_heads, head_dim),
                positions,
            )
            .astype(jnp.bfloat16)
            .reshape(tree_size * group_heads, head_dim)
        )
        request_keys = key_cols[request * tree_size : (request + 1) * tree_size]
        new_keys = (
            rotate(request_keys.astype(jnp.float32).reshape(tree_size, 1, head_dim), positions)
            .astype(jnp.bfloat16)
            .reshape(tree_size, head_dim)
        )
        tree_keys = lax.dynamic_slice_in_dim(new_keys, member * tree_block, tree_block, 0)
        tree_values = lax.dynamic_slice_in_dim(
            value_cols[request * tree_size : (request + 1) * tree_size],
            member * tree_block,
            tree_block,
            0,
        )
        tree_mask = lax.dynamic_slice_in_dim(reached, member * tree_block, tree_block, 1) > 0.5
        cache_mask = jnp.broadcast_to(
            (block_index < cached_length[request])[None, :], (tree_size, block_keys)
        )
        all_keys = jnp.concatenate([cached_key_value[0, request], tree_keys], axis=0)
        all_values = jnp.concatenate([cached_key_value[1, request], tree_values], axis=0)
        blended, row_top, row_total = partial_attention(
            queries,
            all_keys,
            all_values,
            jnp.concatenate([cache_mask, tree_mask], axis=1),
            group_heads,
        )
        value_parts.append(blended.reshape(tree_size, group_width))
        top_parts.append(row_top.reshape(tree_size, group_heads))
        total_parts.append(row_total.reshape(tree_size, group_heads))
    merged = (
        jnp.concatenate(value_parts, axis=0),
        jnp.concatenate(top_parts, axis=0),
        jnp.concatenate(total_parts, axis=0),
    )
    window = group_width // group_size
    zero_offset = jnp.zeros((), jnp.int32)
    for section_bit in range(depth_levels):
        other_state = partner_2(
            (for_sending(merged[0]), for_sending(merged[1]), for_sending(merged[2])),
            "tp",
            section_bit,
        )
        merged = combine(merged, other_state, zero_offset, head_dim)
    offset = member * window
    kept_values = lax.dynamic_slice_in_dim(merged[0], offset, window, 1)
    attention = (kept_values / spread(merged[2], offset, window, head_dim)).astype(jnp.bfloat16)
    summed = lax.psum_scatter(
        jnp.dot(attention, output_weight, preferred_element_type=jnp.float32),
        "tp",
        scatter_dimension=0,
        tiled=True,
    )
    return summed.astype(jnp.bfloat16)


def solution(mesh):
    in_specs = (
        P(("rep", "tp"), None),
        P(),
        P(None, "tp"),
        P(None, "tp"),
        P("tp", None),
        P(None, "rep", "tp", None),
        P("tp", None, None),
        P("tp", None, None),
        P("rep"),
        P(),
        P("rep"),
        P("rep", None),
    )
    out_specs = P(("rep", "tp"), None)
    return jax.shard_map(body, mesh=mesh, in_specs=in_specs, out_specs=out_specs, check_vma=False)
```

profile of v0, /device:TPU:0, one launch (start us, length us, event | category | flops | bytes accessed | tf_op | source)
XLA Modules:
  0.0 312.1 jit_solution(6759295687200955114)
XLA Ops:
  7.3 1.3 fusion.108
  12.2 1.3 fusion.107
  18.5 2.7 select_bitcast_fusion.1
  21.2 0.9 select_bitcast_fusion.3
  22.8 1.2 fusion.78
  28.2 1.0 broadcast_bitcast_fusion.1
  29.3 4.1 %copy.21 = pred[512,4128]{0,1:T(32,128)(4,1)} copy(pred[512,4128]{1,0:T(32,128)(4,1)S(1)} %broadcast_bitcast_fusion.1) | data formatting | bytes 4227072 | tf_op jit(solution)/shard_map/reshape | solution.py:93
  33.5 1.0 broadcast_bitcast_fusion
  34.5 4.2 %copy.24 = pred[512,4128]{0,1:T(32,128)(4,1)} copy(pred[512,4128]{1,0:T(32,128)(4,1)S(1)} %broadcast_bitcast_fusion) | data formatting | bytes 4227072 | tf_op jit(solution)/shard_map/reshape | solution.py:93
  38.7 1.7 slice_bitcast_fusion
  40.7 13.0 %all-gather.2.cloned.1.call-done = bf16[128,8192]{1,0:T(8,128)(2,1)} async-done(((bf16[8,8192]{1,0:T(8,128)(2,1)}), bf16[128,8192]{1,0:T(8,128)(2,1)}) %all-gather.2.cloned.1.call-update) | async-done | bytes 2097168 | tf_op jit(solution)/shard_map/all_gather | solution.py:136
  53.7 2.2 fusion.8
  58.4 97.0 %all-reduce.3.cloned.1.call-done = (bf16[16,10240]{1,0:T(8,128)(2,1)}, bf16[48,8192]{1,0:T(8,128)(2,1)}, bf16[16,10240]{1,0:T(8,128)(2,1)}, bf16[48,8192]{1,0:T(8,128)(2,1)}) async-done(((bf16[16,10240]{1,0:T(8,128)(2,1)}, bf16[48,8192]{1,0:T(8,128)(2,1)}, bf16[16,10240]{1,0:T(8,128)(2,1)}, bf16[48,8192]{1,0:T(8,128)(2,1)}), (bf16[16,10240]{1,0:T(8,128)(2,1)}, bf16[48,8192]{1,0:T(8,128)(2,1)}, ...) | async-done | bytes 2228240 | tf_op jit(solution)/shard_map/psum | solution.py:19
  155.3 2.0 convolution_convert_fusion
  157.4 2.0 convolution_convert_fusion.1
  159.4 0.9 convolution_multiply_fusion
  160.3 0.9 convolution_multiply_fusion.1
  161.2 0.9 fusion.16
  162.1 0.9 fusion.15
  163.0 5.1 %fusion.12 = bf16[64,512]{1,0:T(8,128)(2,1)S(1)} fusion(f32[64,512]{1,0:T(8,128)S(1)} %convolution_multiply_fusion, bf16[8192,512]{1,0:T(8,128)(2,1)} %param.14, bf16[128,8192]{1,0:T(8,128)(2,1)S(1)} %copy-done.5), kind=kOutput, calls=%fused_computation.22 | convolution fusion | flops 536936448 | bytes 9633792 | tf_op jit(solution)/shard_map/dot_general | solution.py:161
  168.1 1.6 fusion.11
  169.8 21.4 %all_gather.7 = bf16[128,2048]{1,0:T(8,128)(2,1)S(1)} all-gather(bf16[128,128]{1,0:T(8,128)(2,1)S(1)} %pad_maximum_fusion.2), channel_id=1, replica_groups=mesh['rep'=2,'tp'=16] {'tp'}, dimensions={1}, use_global_device_ids=true | all-gather | bytes 557056 | tf_op jit(solution)/shard_map/all_gather | solution.py:181
  193.4 5.0 %fusion.112 = (f32[512]{0:T(512)S(1)}, f32[512,4128]{0,1:T(8,128)}) fusion(pred[512,4128]{0,1:T(32,128)(4,1)S(1)} %copy-done.7, bf16[32,128]{1,0:T(8,128)(2,1)S(1)} %get-tuple-element.63, bf16[4096,128]{1,0:T(8,128)(2,1)S(1)} %copy-done.11, bf16[512,64]{1,0:T(8,128)(2,1)S(1)} %get-tuple-element.25, bf16[512,64]{1,0:T(8,128)(2,1)S(1)} %get-tuple-element.24), kind=kOutput, calls=%fused_computation.204 | convolution fusion | flops 549780992 | bytes 11757568 | tf_op jit(solution)/shard_map/dot_general | solution.py:90
  198.5 6.3 %fusion = f32[512]{0:T(512)S(1)} fusion(pred[512,4128]{0,1:T(32,128)(4,1)} %copy.21, f32[512,4128]{0,1:T(8,128)} %get-tuple-element.59, f32[512]{0:T(512)S(1)} %get-tuple-element.58), kind=kLoop, calls=%fused_computation.4 | loop fusion | flops 6340096 | bytes 10571776 | tf_op jit(solution)/shard_map/reduce_sum | solution.py:97
  205.5 2.0 fusion.6
  207.8 6.7 %fusion.111 = (f32[512]{0:T(512)S(1)}, f32[512,4128]{0,1:T(8,128)}) fusion(pred[512,4128]{0,1:T(32,128)(4,1)} %copy.24, bf16[32,128]{1,0:T(8,128)(2,1)S(1)} %get-tuple-element.62, bf16[4096,128]{1,0:T(8,128)(2,1)S(1)} %get-tuple-element.15, bf16[512,64]{1,0:T(8,128)(2,1)S(1)} %get-tuple-element.66, bf16[512,64]{1,0:T(8,128)(2,1)S(1)} %get-tuple-element.67), kind=kOutput, calls=%fused_computation.203 | convolution fusion | flops 549780992 | bytes 11757568 | tf_op jit(solution)/shard_map/dot_general | solution.py:90
  214.6 6.3 %fusion.2 = f32[512]{0:T(512)S(1)} fusion(pred[512,4128]{0,1:T(32,128)(4,1)} %copy.24, f32[512,4128]{0,1:T(8,128)} %get-tuple-element.57, f32[512]{0:T(512)S(1)} %get-tuple-element.56), kind=kLoop, calls=%fused_computation.6 | loop fusion | flops 6340096 | bytes 10571776 | tf_op jit(solution)/shard_map/reduce_sum | solution.py:97
  221.6 2.2 fusion.4
  225.3 0.9 collective-permute-done.3
  227.5 6.7 %fusion.40 = f32[128,8192]{1,0:T(8,128)} fusion(bf16[512,8192]{1,0:T(8,128)(2,1)} %param.16, f32[128,1024]{1,0:T(8,128)S(1)} %bitcast.110, s32[]{:T(128)S(6)} %select_n.187, f32[128,1024]{1,0:T(8,128)S(1)} %bitcast.108, f32[128,1024]{1,0:T(8,128)S(1)} %bitcast.109, f32[128,1024]{1,0:T(8,128)S(1)} %constant_dynamic-update-slice_fusion, ...), kind=kOutput, calls=%fused_computation.91 | convolution fusion | flops 1074135040 | bytes 13762564 | tf_op jit(solution)/shard_map/dot_general | solution.py:259
  234.2 69.7 %reduce-scatter.2.cloned.1.call-done = f32[8,8192]{1,0:T(8,128)} async-done(((f32[128,8192]{1,0:T(8,128)}), f32[8,8192]{1,0:T(8,128)}) %reduce-scatter.2.cloned.1.call-update) | async-done | bytes 262160 | tf_op jit(solution)/shard_map/reduce_scatter | solution.py:258
  303.9 1.6 convert_element_type.147
  (121 shorter events, 15.1 us)
Async XLA Ops:
  6.5 50.0 %copy-start = (bf16[8192,128]{1,0:T(8,128)(2,1)S(1)}, bf16[8192,128]{1,0:T(8,128)(2,1)}, u32[]{:S(2)}) copy-start(bf16[8192,128]{1,0:T(8,128)(2,1)} %param.15) | copy-start | bytes 6291460
  6.5 14.7 %copy-start.14 = (bf16[2,16,10240]{2,1,0:T(8,128)(2,1)S(1)}, bf16[2,16,10240]{2,1,0:T(8,128)(2,1)}, u32[]{:S(2)}) copy-start(bf16[2,16,10240]{2,1,0:T(8,128)(2,1)} %param.19) | copy-start | bytes 1966084
  6.5 47.1 %all-gather.2.cloned.1.call-start = ((), (), s32[]{:S(2)}) async-start(), calls=%async_computation.1 | async-start | bytes 2228224 | tf_op jit(solution)/shard_map/all_gather | solution.py:136
  7.3 148.1 %all-reduce.3.cloned.1.call-start = ((), (), s32[]{:S(2)}) async-start(), calls=%async_computation.3 | async-start | bytes 4456448 | tf_op jit(solution)/shard_map/psum | solution.py:19
  21.2 1.1 copy-start.17
  21.2 1.6 copy-start.18
  22.1 281.8 %reduce-scatter.2.cloned.1.call-start = ((), (), s32[]{:S(2)}) async-start(), calls=%async_computation.2 | async-start | bytes 4456448 | tf_op jit(solution)/shard_map/reduce_scatter | solution.py:258
  34.5 4.2 %copy-start.10 = (bf16[2,2,4096,128]{3,2,1,0:T(8,128)(2,1)S(1)}, bf16[2,2,4096,128]{3,2,1,0:T(8,128)(2,1)}, u32[]{:S(2)}) copy-start(bf16[2,2,4096,128]{3,2,1,0:T(8,128)(2,1)} %param.17) | copy-start | bytes 12582916
  40.4 15.5 %copy-start.15 = (f32[8192]{0:T(1024)S(1)}, f32[8192]{0:T(1024)}, u32[]{:S(2)}) copy-start(f32[8192]{0:T(1024)} %param.13) | copy-start | bytes 98308
  53.6 2.3 copy-start.9
  56.5 1.4 copy-start.4
  155.3 7.6 %copy-start.5 = (bf16[128,8192]{1,0:T(8,128)(2,1)S(1)}, bf16[128,8192]{1,0:T(8,128)(2,1)}, u32[]{:S(2)}) copy-start(bf16[128,8192]{1,0:T(8,128)(2,1)} %copy-done.4) | copy-start | bytes 6291460
  157.4 10.7 %slice-start = ((s8[8388608]{0:T(1024)(128)(4,1)}), s8[4194304]{0:T(1024)(128)(4,1)S(1)}, s32[]{:S(2)}) async-start(s8[8388608]{0:T(1024)(128)(4,1)} %bitcast.101), calls=%async_computation.4 | async-start | bytes 8388608
  163.0 5.1 %slice-start.1 = ((s8[8388608]{0:T(1024)(128)(4,1)}), s8[4194304]{0:T(1024)(128)(4,1)S(1)}, s32[]{:S(2)}) async-start(s8[8388608]{0:T(1024)(128)(4,1)} %bitcast.101), calls=%async_computation.5 | async-start | bytes 8388608
  169.7 22.5 %collective-permute-start = (bf16[128,512]{1,0:T(8,128)(2,1)S(1)}, bf16[128,512]{1,0:T(8,128)(2,1)S(1)}, u32[]{:S(2)}, u32[]{:S(2)}) collective-permute-start(bf16[128,512]{1,0:T(8,128)(2,1)S(1)} %pad_maximum_fusion.1), channel_id=1, source_target_pairs={{0,1},{1,0},{2,3},{3,2},{4,5},{5,4},{6,7},{7,6},{8,9},{9,8},{10,11... | collective-permute-start | bytes 393224 | tf_op jit(solution)/shard_map/ppermute | solution.py:25
  191.5 1.6 copy-start.7
  191.5 1.9 copy-start.11
  193.4 11.4 %copy-start.13 = (bf16[4096,128]{1,0:T(8,128)(2,1)S(1)}, bf16[4096,128]{1,0:T(8,128)(2,1)}, u32[]{:S(2)}) copy-start(bf16[4096,128]{1,0:T(8,128)(2,1)} %get-tuple-element.13) | copy-start | bytes 3145732
  193.4 11.4 %copy-start.16 = (bf16[32,128]{1,0:T(8,128)(2,1)S(1)}, bf16[32,128]{1,0:T(8,128)(2,1)}, u32[]{:S(2)}) copy-start(bf16[32,128]{1,0:T(8,128)(2,1)} %get-tuple-element.21) | copy-start | bytes 24580
  198.5 6.4 %copy-start.3 = (f32[512,4128]{0,1:T(8,128)S(1)}, f32[512,4128]{0,1:T(8,128)}, u32[]{:S(2)}) copy-start(f32[512,4128]{0,1:T(8,128)} %get-tuple-element.59) | copy-start | bytes 25362436
  198.5 7.0 %copy-start.8 = (pred[512,4128]{0,1:T(32,128)(4,1)S(1)}, pred[512,4128]{0,1:T(32,128)(4,1)}, u32[]{:S(2)}) copy-start(pred[512,4128]{0,1:T(32,128)(4,1)} %copy.21) | copy-start | bytes 6340612
  207.8 13.1 %copy-start.12 = (bf16[4096,128]{1,0:T(8,128)(2,1)S(1)}, bf16[4096,128]{1,0:T(8,128)(2,1)}, u32[]{:S(2)}) copy-start(bf16[4096,128]{1,0:T(8,128)(2,1)} %get-tuple-element.12) | copy-start | bytes 3145732
  214.6 6.4 %copy-start.2 = (f32[512,4128]{0,1:T(8,128)S(1)}, f32[512,4128]{0,1:T(8,128)}, u32[]{:S(2)}) copy-start(f32[512,4128]{0,1:T(8,128)} %get-tuple-element.57) | copy-start | bytes 25362436
  214.6 7.0 %copy-start.6 = (pred[512,4128]{0,1:T(32,128)(4,1)S(1)}, pred[512,4128]{0,1:T(32,128)(4,1)}, u32[]{:S(2)}) copy-start(pred[512,4128]{0,1:T(32,128)(4,1)} %copy.24) | copy-start | bytes 6340612
  224.0 1.2 collective-permute-start.1
  224.6 2.9 collective-permute-start.2
  224.9 1.3 collective-permute-start.3
  234.2 71.3 %copy-start.1 = (bf16[8192,128]{1,0:T(8,128)(2,1)S(1)}, bf16[8192,128]{1,0:T(8,128)(2,1)}, u32[]{:S(2)}) copy-start(bf16[8192,128]{1,0:T(8,128)(2,1)} %param.15) | copy-start | bytes 6291460
Sparse Core Ops, SparseCore 0:
  9.5 44.0 all-gather.1
  57.6 97.7 all-reduce.2
  234.3 69.5 reduce-scatter.1
where the time goes:
time: 313 us; the launch traced here: 312 us
  waiting for transfers between devices  181 us (58%)
  matrix products  40.4 us (13%)
  other arithmetic  24.7 us (8%)
  between operations  22.3 us (7%)
  blocking collectives  21.4 us (7%)
  local copies, waits for them, and re-layouts  20.9 us (7%)
    psum x1, waiting for transfers between devices, broadcast(): return lax.psum(block, axis)  97 us
    reduce_scatter x1, waiting for transfers between devices, body(): lax.psum_scatter(jnp.dot(attention, output_weight, preferred_element_type...  69.7 us
    all_gather x1, blocking collectives, body(): pair_all = lax.all_gather(pair_local, 'tp', axis=1, tiled=True)  21.4 us
    all_gather x1, waiting for transfers between devices, body(): everyone = lax.all_gather(layer_input, 'tp', axis=0, tiled=True)  13 us
    reduce_sum x2, other arithmetic, partial_attention(): row_total = jnp.sum(weights, axis=1, keepdims=True)  12.6 us
    dot_general x2, matrix products, partial_attention(): lax.dot_general(queries, all_keys, (((1,), (1,)), ((), ())), preferred_el...  11.7 us
    reshape x4, local copies, waits for them, and re-layouts, partial_attention(): mask_rows = jnp.repeat(usable, group_heads, axis=0)  10.3 us
    dot_general x1, matrix products, body(): jnp.dot(attention, output_weight, preferred_element_type=jnp.float32)  6.66 us
  transfers between devices with their start and end apart: 7, of which 4 were waited for; matrix products, arithmetic and copies ran while one was open for 10% of the time, Pallas kernels for 0%

commit v1 on v0

--- a/solution.py
+++ b/solution.py
@@ -3,6 +3,8 @@
 import jax
 import jax.numpy as jnp
 from jax import lax
+from jax.experimental import pallas as pl
+from jax.experimental.pallas import tpu as pltpu
 from jax.sharding import PartitionSpec as P
 
 KEY_HEADS = 8
@@ -264,6 +266,422 @@
     return summed.astype(jnp.bfloat16)
 
 
+MESH = pl.DeviceIdType.MESH
+LINE, PAIR, CORES = 4, 2, 2
+OUT_CHUNKS = 4
+KEY_CHUNK = 1024
+lowest = -1e29
+
+
+def fused_kernel(
+    slot_of, adapter_of, length_of, rows_in, gain, parents, inverse, down, up,
+    query_weight, pair_weight, out_weight, cache, out,
+    w_query, w_pair, w_out, kv_cache, rows_all, normed, down_here, up_here,
+    up_send, up_sib, up_mid, up_y, up_low, up_z, low_send, low_recv,
+    query_buf, pair_own, tree_keys, tree_values, blended, tops, totals,
+    merge_send, merge_recv, attention, part, part_sib, y_send, y_recv, z_send, z_recv,
+    load_sem, rows_send, rows_recv, up_ssem, up_rsem, low_ssem, low_rsem,
+    query_sem, pair_ssem, pair_rsem, merge_ssem, merge_rsem,
+    sib_ssem, sib_rsem, y_ssem, y_rsem, z_ssem, z_rsem,
+):
+    me = lax.axis_index("tp")
+    z, y, c = me // (PAIR * CORES), me // CORES % PAIR, me % CORES
+    count = LINE * PAIR * CORES
+
+    def at(zz, yy, cc):
+        return (zz * PAIR + yy) * CORES + cc
+
+    def hop(k):
+        return (z + k) % LINE
+
+    def remote(src, dst, ssem, rsem, target):
+        return pltpu.make_async_remote_copy(
+            src_ref=src, dst_ref=dst, send_sem=ssem, recv_sem=rsem,
+            device_id={"tp": target}, device_id_type=MESH,
+        )
+
+    sib, ypart = at(z, y, 1 - c), at(z, 1 - y, c)
+    loads = [
+        pltpu.make_async_copy(a, b, load_sem.at[i])
+        for i, (a, b) in enumerate([
+            (up, up_here), (down, down_here), (query_weight, w_query),
+            (pair_weight, w_pair), (cache, kv_cache), (out_weight, w_out)])
+    ]
+    for load in loads:
+        load.start()
+    barrier = pltpu.get_barrier_semaphore()
+    for k in range(1, count):
+        pl.semaphore_signal(
+            barrier, inc=1, device_id={"tp": (me + k) % count}, device_id_type=MESH)
+    rows_all[me] = rows_in[...]
+    pl.semaphore_wait(barrier, count - 1)
+
+    sent = []
+
+    def push_rows(block, target):
+        copy = remote(rows_all.at[block], rows_all.at[block],
+                      rows_send.at[len(sent)], rows_recv.at[block], target)
+        copy.start()
+        sent.append(copy)
+
+    def take_rows(block):
+        remote(rows_all.at[block], rows_all.at[block], rows_send.at[0],
+               rows_recv.at[block], sib).wait_recv()
+
+    for k in range(1, LINE):
+        push_rows(me, at(hop(k), y, c))
+    push_rows(me, ypart)
+    push_rows(me, sib)
+
+    requests, tree = 2, 64
+    rank, slots = up_here.shape[1], up_here.shape[0]
+    q_cols, p_cols = w_query.shape[1], w_pair.shape[1]
+    width = q_cols * count
+    chosen = []
+    for r in range(requests):
+        slot = slot_of[adapter_of[r]]
+        chosen.append([slot == me * slots + s for s in range(slots)])
+    loads[0].wait()
+    for r in range(requests):
+        picked = jnp.zeros(up_here.shape[1:], up_here.dtype)
+        for s in range(slots):
+            picked = jnp.where(chosen[r][s], up_here[s], picked)
+        for d in range(count):
+            zz, yy, cc = d // 4, d // 2 % 2, d % 2
+            up_send[cc, yy, zz, r * rank:(r + 1) * rank, :q_cols] = (
+                picked[:, d * q_cols:(d + 1) * q_cols])
+            up_send[cc, yy, zz, r * rank:(r + 1) * rank, q_cols:] = (
+                picked[:, width + d * p_cols:width + (d + 1) * p_cols])
+    up_first = remote(up_send.at[1 - c], up_sib, up_ssem.at[0], up_rsem.at[0], sib)
+    up_first.start()
+
+    for k in range(1, LINE):
+        block = at(hop(k), y, c)
+        take_rows(block)
+        push_rows(block, ypart)
+        push_rows(block, sib)
+
+    up_first.wait()
+    up_mid[...] = up_send[c] + up_sib[...]
+    up_second = remote(up_mid.at[1 - y], up_y, up_ssem.at[1], up_rsem.at[1], ypart)
+    up_second.start()
+
+    reached, cosines, sines = [], [], []
+    node = lax.broadcasted_iota(jnp.int32, (tree, tree), 1)
+    own = lax.broadcasted_iota(jnp.int32, (tree, tree), 0)
+    for r in range(requests):
+        hot = jnp.where((parents[r] == node) | (own == node), 1.0, 0.0)
+        for _ in range(tree.bit_length()):
+            short = hot.astype(jnp.bfloat16)
+            hot = jnp.minimum(
+                jnp.dot(short, short, preferred_element_type=jnp.float32), 1.0)
+        reached.append(hot)
+        depth = jnp.sum(hot, axis=1, keepdims=True).astype(jnp.int32) - 1
+        position = (depth + length_of[r]).astype(jnp.float32)
+        angles = position * inverse[...]
+        cosines.append(jnp.cos(angles))
+        sines.append(jnp.sin(angles))
+
+    for k in range(LINE):
+        block = at(hop(k), 1 - y, c)
+        take_rows(block)
+        push_rows(block, sib)
+
+    up_second.wait()
+    up_low[...] = up_mid[y] + up_y[...]
+    up_third = []
+    for k in range(1, LINE):
+        copy = remote(up_low.at[hop(k)], up_z.at[k - 1], up_ssem.at[1 + k], up_rsem.at[1 + k],
+                      at(hop(k), y, c))
+        copy.start()
+        up_third.append(copy)
+
+    for k in range(LINE):
+        for yy in (y, 1 - y):
+            take_rows(at(hop(k), yy, 1 - c))
+
+    half = rows_all.shape[2]
+
+    def norm_step(k, carry):
+        parts = []
+        for j in range(2):
+            block = rows_all[2 * k + j].astype(jnp.float32)
+            squares = jnp.sum(block * block, axis=1, keepdims=True)
+            scale = lax.rsqrt((squares[:8] + squares[8:]) / (2 * half) + epsilon)
+            parts.append((block[:8] * scale, block[8:] * scale))
+        for h in range(2):
+            both = jnp.concatenate([parts[0][h], parts[1][h]], axis=0)
+            cols = slice(h * half, (h + 1) * half)
+            normed[pl.ds(pl.multiple_of(k * 16, 16), 16), cols] = (
+                both * gain[:, cols]).astype(jnp.bfloat16)
+        return carry
+
+    lax.fori_loop(0, count // 2, norm_step, 0)
+
+    nt = (((1,), (1,)), ((), ()))
+    tn = (((0,), (0,)), ((), ()))
+    loads[1].wait()
+    token = lax.broadcasted_iota(jnp.int32, (1, requests * tree), 1)
+    low = jnp.zeros((down_here.shape[1], requests * tree), jnp.float32)
+    for s in range(slots):
+        flag = jnp.where(token < tree, chosen[0][s].astype(jnp.int32),
+                         chosen[1][s].astype(jnp.int32))
+        value = lax.dot_general(down_here[s], normed[...], nt,
+                                preferred_element_type=jnp.float32)
+        low = jnp.where(flag == 1, value, low)
+    low_send[0] = low.astype(jnp.bfloat16)
+    first = remote(low_send.at[0], low_recv.at[0], low_ssem.at[0], low_rsem.at[0], sib)
+    first.start()
+
+    loads[2].wait()
+    loads[3].wait()
+    steps = 4
+    depth = w_query.shape[0] // steps
+    q_acc = jnp.zeros((requests * tree, q_cols), jnp.float32)
+    p_acc = jnp.zeros((requests * tree, p_cols), jnp.float32)
+    pending = first
+    thirds = []
+    for step in range(steps):
+        cut = slice(step * depth, (step + 1) * depth)
+        q_acc += jnp.dot(normed[:, cut], w_query[cut], preferred_element_type=jnp.float32)
+        p_acc += jnp.dot(normed[:, cut], w_pair[cut], preferred_element_type=jnp.float32)
+        if step == 0:
+            first.wait()
+            low_send[1] = low_send[0] + low_recv[0]
+            second = remote(low_send.at[1], low_recv.at[1], low_ssem.at[1], low_rsem.at[1], ypart)
+            second.start()
+        if step == 1:
+            second.wait()
+            low_send[2] = low_send[1] + low_recv[1]
+            for k in range(1, LINE):
+                copy = remote(low_send.at[2], low_recv.at[1 + k], low_ssem.at[1 + k],
+                              low_rsem.at[1 + k], at(hop(k), y, c))
+                copy.start()
+                thirds.append(copy)
+    for copy in thirds + up_third:
+        copy.wait()
+    low_all = low_send[2] + low_recv[2] + low_recv[3] + low_recv[4]
+    up_all = up_low[z] + up_z[0] + up_z[1] + up_z[2]
+    is_value = me >= count // 2
+    q_heads = q_cols // 128
+
+    def rotated(vectors, r):
+        front, back = vectors[:, :tree], vectors[:, tree:]
+        return jnp.concatenate(
+            [front * cosines[r] - back * sines[r], back * cosines[r] + front * sines[r]], axis=1)
+
+    for r in range(requests):
+        rows = slice(r * tree, (r + 1) * tree)
+        low_r = low_all[:, rows]
+        up_r = up_all[r * rank:(r + 1) * rank]
+        update = lax.dot_general(low_r[:rank], up_r[:, :q_cols], tn,
+                                 preferred_element_type=jnp.float32)
+        q_pre = (q_acc[rows] + adapter_scale * update).astype(jnp.bfloat16).astype(jnp.float32)
+        for h in range(q_heads):
+            query_buf[c, r, h] = rotated(q_pre[:, h * 128:(h + 1) * 128], r).astype(jnp.bfloat16)
+        pair_low = jnp.where(is_value, low_r[2 * rank:], low_r[rank:2 * rank])
+        update = lax.dot_general(pair_low, up_r[:, q_cols:], tn,
+                                 preferred_element_type=jnp.float32)
+        p_pre = (p_acc[rows] + adapter_scale * update).astype(jnp.bfloat16).astype(jnp.float32)
+        final = jnp.where(is_value, p_pre, rotated(p_pre, r)).astype(jnp.bfloat16)
+        for m in range(CORES):
+            pair_own[m, r] = final[m * (tree // 2):(m + 1) * (tree // 2)]
+
+    q_copy = remote(query_buf.at[c], query_buf.at[c], query_sem.at[0], query_sem.at[1], sib)
+    q_copy.start()
+    group = me % (count // 2)
+    for is_v, landing in ((0, tree_keys), (1, tree_values)):
+        for m in range(CORES):
+            target = group * CORES + m
+
+            @pl.when((is_value == (is_v == 1)) & (target != me))
+            def _():
+                remote(pair_own.at[m], landing, pair_ssem.at[m], pair_rsem.at[is_v], target).start()
+
+            @pl.when((is_value == (is_v == 1)) & (target == me))
+            def _():
+                landing[...] = pair_own[m]
+
+    for m in range(CORES):
+        @pl.when(group * CORES + m != me)
+        def _():
+            remote(pair_own.at[m], tree_keys, pair_ssem.at[m], pair_rsem.at[0], sib).wait_send()
+
+    @pl.when(me // CORES != me)
+    def _():
+        remote(pair_own.at[0], tree_keys, pair_ssem.at[0], pair_rsem.at[0], sib).wait_recv()
+
+    @pl.when(me // CORES + count // 2 != me)
+    def _():
+        remote(pair_own.at[0], tree_values, pair_ssem.at[0], pair_rsem.at[1], sib).wait_recv()
+
+    q_copy.wait_send()
+    remote(query_buf.at[1 - c], query_buf.at[1 - c], query_sem.at[0], query_sem.at[1],
+           sib).wait_recv()
+    for copy in sent:
+        copy.wait_send()
+
+    loads[4].wait()
+    heads = CORES * q_heads
+    block_rows = heads * tree
+    scale = 128 ** -0.5
+    slots_here = kv_cache.shape[2]
+    for r in range(requests):
+        queries = query_buf[:, r].reshape(block_rows, 128)
+        mask = jnp.where(c == 0, reached[r][:, :tree // 2], reached[r][:, tree // 2:])
+        mask = jnp.concatenate([mask] * heads, axis=0)
+        scores = lax.dot_general(queries, tree_keys[r], nt,
+                                 preferred_element_type=jnp.float32) * scale
+        scores = jnp.where(mask > 0.5, scores, masked_score)
+        top = jnp.maximum(jnp.max(scores, axis=1, keepdims=True), lowest)
+        weights = jnp.exp(scores - top)
+        total = jnp.sum(weights, axis=1, keepdims=True)
+        blend = jnp.dot(weights.astype(jnp.bfloat16), tree_values[r],
+                        preferred_element_type=jnp.float32)
+        limit = length_of[r] - c * slots_here
+
+        def key_step(j, carry):
+            top, total, blend = carry
+            start = pl.multiple_of(j * KEY_CHUNK, KEY_CHUNK)
+            scores = lax.dot_general(queries, kv_cache[0, r, pl.ds(start, KEY_CHUNK)], nt,
+                                     preferred_element_type=jnp.float32) * scale
+            column = lax.broadcasted_iota(jnp.int32, (1, KEY_CHUNK), 1) + start
+            scores = jnp.where(column < limit, scores, masked_score)
+            new_top = jnp.maximum(top, jnp.max(scores, axis=1, keepdims=True))
+            weights = jnp.exp(scores - new_top)
+            factor = jnp.exp(top - new_top)
+            total = total * factor + jnp.sum(weights, axis=1, keepdims=True)
+            blend = blend * factor + jnp.dot(
+                weights.astype(jnp.bfloat16), kv_cache[1, r, pl.ds(start, KEY_CHUNK)],
+                preferred_element_type=jnp.float32)
+            return new_top, total, blend
+
+        top, total, blend = lax.fori_loop(0, slots_here // KEY_CHUNK, key_step,
+                                          (top, total, blend))
+        top = jnp.broadcast_to(top, blend.shape)
+        total = jnp.broadcast_to(total, blend.shape)
+        mine = block_rows // CORES
+        for m in range(CORES):
+            cut = slice(m * mine, (m + 1) * mine)
+            merge_send[m, r, 0] = blend[cut]
+            merge_send[m, r, 1] = top[cut]
+            merge_send[m, r, 2] = total[cut]
+        remote(merge_send.at[1 - c, r], merge_recv.at[r], merge_ssem.at[r], merge_rsem.at[r],
+               sib).start()
+
+    loads[5].wait()
+    for r in range(requests):
+        remote(merge_send.at[1 - c, r], merge_recv.at[r], merge_ssem.at[r], merge_rsem.at[r],
+               sib).wait()
+        top = jnp.maximum(merge_send[c, r, 1], merge_recv[r, 1])
+        f_own, f_other = jnp.exp(merge_send[c, r, 1] - top), jnp.exp(merge_recv[r, 1] - top)
+        total = merge_send[c, r, 2] * f_own + merge_recv[r, 2] * f_other
+        value = (merge_send[c, r, 0] * f_own + merge_recv[r, 0] * f_other) / total
+        value = value.astype(jnp.bfloat16)
+        for h in range(q_heads):
+            attention[r * tree:(r + 1) * tree, h * 128:(h + 1) * 128] = (
+                value[h * tree:(h + 1) * tree])
+
+    columns = w_out.shape[1] // OUT_CHUNKS
+
+    def sib_copy(n):
+        return remote(part.at[n, 1 - c], part_sib.at[n], sib_ssem.at[n], sib_rsem.at[n], sib)
+
+    def y_copy(n):
+        return remote(y_send.at[n], y_recv.at[n], y_ssem.at[n], y_rsem.at[n], ypart)
+
+    def z_copy(n, k):
+        return remote(z_send.at[n, hop(k)], z_recv.at[n, k - 1], z_ssem.at[n, k - 1],
+                      z_rsem.at[n, k - 1], at(hop(k), y, c))
+
+    for n in range(OUT_CHUNKS):
+        product = jnp.dot(attention[...], w_out[:, n * columns:(n + 1) * columns],
+                          preferred_element_type=jnp.float32)
+        for d in range(count):
+            part[n, d % 2, d // 2 % 2, d // 4] = product[d * 8:(d + 1) * 8]
+        sib_copy(n).start()
+    for n in range(OUT_CHUNKS):
+        sib_copy(n).wait()
+        away = part[n, c, 1 - y] + part_sib[n, 1 - y]
+        y_send[n] = away.reshape(LINE * 8, columns).astype(jnp.bfloat16)
+        y_copy(n).start()
+    for n in range(OUT_CHUNKS):
+        y_copy(n).wait()
+        held = (part[n, c, y] + part_sib[n, y]) + y_recv[n].astype(jnp.float32).reshape(
+            LINE, 8, columns)
+        part_sib[n, 0] = held
+        for d in range(LINE):
+            z_send[n, d] = jnp.concatenate(
+                [held[d, :, :columns // 2], held[d, :, columns // 2:]], axis=0).astype(jnp.bfloat16)
+        for k in range(1, LINE):
+            z_copy(n, k).start()
+    for n in range(OUT_CHUNKS):
+        total = part_sib[n, 0, z]
+        for k in range(1, LINE):
+            z_copy(n, k).wait()
+            landed = z_recv[n, k - 1].astype(jnp.float32)
+            total = total + jnp.concatenate([landed[:8], landed[8:]], axis=1)
+        out[:, n * columns:(n + 1) * columns] = total.astype(jnp.bfloat16)
+
+
+def fused_body(
+    layer_input, input_norm_gain, query_weight, key_value_weight, output_weight,
+    cached_key_value, adapter_down_weight, adapter_up_weight, request_adapter,
+    adapter_storage_index, cached_length, parent_node,
+):
+    rows, model = layer_input.shape
+    half = model // 2
+    packed = layer_input.reshape(rows, 2, half).transpose(1, 0, 2).reshape(2 * rows, half)
+    exponents = jnp.arange(64, dtype=jnp.float32) * (2.0 / 128)
+    inverse = jnp.exp(exponents * -math.log(rope_base))[None]
+    bf, f32 = jnp.bfloat16, jnp.float32
+    count = 16
+    rank = adapter_up_weight.shape[1]
+    ranks = adapter_down_weight.shape[1]
+    cols = query_weight.shape[1] + key_value_weight.shape[1]
+    columns = model // OUT_CHUNKS
+    dma = pltpu.SemaphoreType.DMA
+    n = OUT_CHUNKS
+    scratch = [
+        pltpu.VMEM(query_weight.shape, bf), pltpu.VMEM(key_value_weight.shape, bf),
+        pltpu.VMEM(output_weight.shape, bf), pltpu.VMEM(cached_key_value.shape, bf),
+        pltpu.VMEM((count, 2 * rows, half), bf), pltpu.VMEM((count * rows, model), bf),
+        pltpu.VMEM(adapter_down_weight.shape, bf), pltpu.VMEM(adapter_up_weight.shape, bf),
+        pltpu.VMEM((2, 2, 4, 2 * rank, cols), bf), pltpu.VMEM((2, 4, 2 * rank, cols), bf),
+        pltpu.VMEM((2, 4, 2 * rank, cols), bf), pltpu.VMEM((4, 2 * rank, cols), bf),
+        pltpu.VMEM((4, 2 * rank, cols), bf), pltpu.VMEM((3, 2 * rank, cols), bf),
+        pltpu.VMEM((3, ranks, 128), bf), pltpu.VMEM((5, ranks, 128), bf),
+        pltpu.VMEM((2, 2, 4, 64, 128), bf), pltpu.VMEM((2, 2, 32, 128), bf),
+        pltpu.VMEM((2, 32, 128), bf), pltpu.VMEM((2, 32, 128), bf),
+        pltpu.VMEM((8, 128), f32), pltpu.VMEM((8, 128), f32), pltpu.VMEM((8, 128), f32),
+        pltpu.VMEM((2, 2, 3, 256, 128), f32), pltpu.VMEM((2, 3, 256, 128), f32),
+        pltpu.VMEM((128, 512), bf),
+        pltpu.VMEM((n, 2, 2, 4, 8, columns), f32), pltpu.VMEM((n, 2, 4, 8, columns), f32),
+        pltpu.VMEM((n, 32, columns), bf), pltpu.VMEM((n, 32, columns), bf),
+        pltpu.VMEM((n, 4, 16, columns // 2), bf), pltpu.VMEM((n, 3, 16, columns // 2), bf),
+        dma((6,)), dma((15,)), dma((count,)), dma((5,)), dma((5,)), dma((5,)), dma((5,)),
+        dma((2,)), dma((2,)), dma((2,)), dma((2,)), dma((2,)),
+        dma((n,)), dma((n,)), dma((n,)), dma((n,)), dma((n, 3)), dma((n, 3)),
+    ]
+    smem = pl.BlockSpec(memory_space=pltpu.SMEM)
+    vmem = pl.BlockSpec(memory_space=pltpu.VMEM)
+    hbm = pl.BlockSpec(memory_space=pl.ANY)
+    return pl.pallas_call(
+        fused_kernel,
+        out_shape=jax.ShapeDtypeStruct((rows, model), bf),
+        in_specs=[smem] * 3 + [vmem] * 4 + [hbm] * 6,
+        out_specs=vmem,
+        scratch_shapes=scratch,
+        compiler_params=pltpu.CompilerParams(
+            collective_id=0, has_side_effects=True, vmem_limit_bytes=60 * 2**20),
+        cost_estimate=pl.CostEstimate(
+            flops=5 * 10**9, bytes_accessed=25 * 2**20, transcendentals=4 * 2**20),
+        name="fused_layer",
+    )(adapter_storage_index, request_adapter, cached_length, packed, input_norm_gain[None],
+      parent_node[:, :, None], inverse, adapter_down_weight, adapter_up_weight,
+      query_weight, key_value_weight, output_weight, cached_key_value)
+
+
 def solution(mesh):
     in_specs = (
         P(("rep", "tp"), None),
@@ -280,4 +698,5 @@
         P("rep", None),
     )
     out_specs = P(("rep", "tp"), None)
-    return jax.shard_map(body, mesh=mesh, in_specs=in_specs, out_specs=out_specs, check_vma=False)
+    fused = mesh.shape["tp"] == 16 and mesh.shape["rep"] == 2
+    return jax.shard_map(fused_body if fused else body, mesh=mesh, in_specs=in_specs, out_specs=out_specs, check_vma=False)

time: 313 us -> 81.9 us (0.26)
  waiting for transfers between devices: 181 us -> 0 us
  Pallas kernels: 0 us -> 78.2 us
  matrix products: 40.4 us -> 0 us
  other arithmetic: 24.7 us -> 0.52 us
  between operations: 22.3 us -> 0.01 us
  blocking collectives: 21.4 us -> 0 us
  local copies, waits for them, and re-layouts: 20.9 us -> 2.98 us
    psum x1 -> x0, waiting for transfers between devices: 97 us -> none  [broadcast(): return lax.psum(block, axis)]
    pallas_call x0 -> x1, Pallas kernels: none -> 78.2 us  [fused_body(): pl.pallas_call(fused_kernel, out_shape=jax.ShapeDtypeStruct((rows, model)...]
    reduce_scatter x1 -> x0, waiting for transfers between devices: 69.7 us -> none  [body(): lax.psum_scatter(jnp.dot(attention, output_weight, preferred_element_type...]
    dot_general x29 -> x0, matrix products: 40.4 us -> none  [the longest x2 11.7 us: partial_attention(): lax.dot_general(queries, all_keys, (((1,), (1,)), ((), ())), preferred_el...]
    all_gather x1 -> x0, blocking collectives: 21.4 us -> none  [body(): pair_all = lax.all_gather(pair_local, 'tp', axis=1, tiled=True)]
    reduce_sum x3 -> x0, other arithmetic: 14.8 us -> none  [the longest x2 12.6 us: partial_attention(): row_total = jnp.sum(weights, axis=1, keepdims=True)]
    all_gather x1 -> x0, waiting for transfers between devices: 13 us -> none  [body(): everyone = lax.all_gather(layer_input, 'tp', axis=0, tiled=True)]
    reshape x6 -> x0, local copies, waits for them, and re-layouts: 10.4 us -> none  [the longest x4 10.3 us: partial_attention(): mask_rows = jnp.repeat(usable, group_heads, axis=0)]
  transfers between devices with their start and end apart: 7 -> 0, of which waited for: 4 -> 0; matrix products, arithmetic and copies ran while one was open for 10% -> 0% of each run, Pallas kernels for 0% -> 0%
where the time goes in v1:
time: 81.9 us; the launch traced here: 81.7 us
  Pallas kernels  78.2 us (95%)
  local copies, waits for them, and re-layouts  2.98 us (4%)
    pallas_call x1, Pallas kernels, fused_body(): pl.pallas_call(fused_kernel, out_shape=jax.ShapeDtypeStruct((rows, model)...  78.2 us

profile of v1, /device:TPU:0, one launch (start us, length us, event | category | flops | bytes accessed | tf_op | source)
XLA Modules:
  0.0 81.7 jit_solution(3763309993266544688)
XLA Ops:
  0.0 0.5 multiply_exponential_fusion.inverse
  0.5 1.4 %copy.13.parents = s32[2,64,1]{2,1,0:T(8,128)} copy(s32[2,64,1]{1,0,2:T(2,128)} %bitcast.9) | data formatting | bytes 1024 | tf_op jit(solution)/shard_map/broadcast_in_dim | solution.py:681
  1.9 78.2 %fused_layer.1 = bf16[8,8192]{1,0:T(8,128)(2,1)} custom-call(s32[32]{0:T(128)} %slot_of.1, s32[2]{0:T(128)} %adapter_of.1, s32[2]{0:T(128)} %length_of.1, bf16[16,4096]{1,0:T(8,128)(2,1)} %bitcast.7, f32[1,8192]{1,0:T(1,128)} %bitcast.8, s32[2,64,1]{2,1,0:T(8,128)} %copy.13.parents, f32[1,64]{1,0:T(1,128)} %multiply_exponential_fusion.inverse, ...), custom_call_target="tpu_custom_call" | custom-call | flops 5000000000 | bytes 26214400 | tf_op jit(solution)/shard_map/fused_layer/pallas_call | solution.py:669
  80.1 1.6 %copy.15 = bf16[8,8192]{1,0:T(8,128)(2,1)} copy(bf16[8,8192]{1,0:T(8,128)(2,1)} %fused_layer.1) | data formatting | bytes 262144

commit v2 on v1

--- a/solution.py
+++ b/solution.py
@@ -1,6 +1,7 @@
 import math
 
 import jax
+import numpy as np
 import jax.numpy as jnp
 from jax import lax
 from jax.experimental import pallas as pl
@@ -278,9 +279,9 @@
     query_weight, pair_weight, out_weight, cache, out,
     w_query, w_pair, w_out, kv_cache, rows_all, normed, down_here, up_here,
     up_send, up_sib, up_mid, up_y, up_low, up_z, low_send, low_recv,
-    query_buf, pair_own, tree_keys, tree_values, blended, tops, totals,
+    query_buf, pair_own, tree_keys, tree_values,
     merge_send, merge_recv, attention, part, part_sib, y_send, y_recv, z_send, z_recv,
-    load_sem, rows_send, rows_recv, up_ssem, up_rsem, low_ssem, low_rsem,
+    load_sem, rows_send, line_send, rows_recv, up_ssem, up_rsem, low_ssem, low_rsem,
     query_sem, pair_ssem, pair_rsem, merge_ssem, merge_rsem,
     sib_ssem, sib_rsem, y_ssem, y_rsem, z_ssem, z_rsem,
 ):
@@ -328,8 +329,24 @@
         remote(rows_all.at[block], rows_all.at[block], rows_send.at[0],
                rows_recv.at[block], sib).wait_recv()
 
-    for k in range(1, LINE):
-        push_rows(me, at(hop(k), y, c))
+    def line_copy(distance, side):
+        block = at(z - side * distance, y, c)
+        return remote(rows_all.at[block], rows_all.at[block],
+                      line_send.at[distance, (side + 1) // 2, 0], rows_recv.at[block],
+                      at(z + side, y, c))
+
+    def fan_copy(distance, side, target, place):
+        block = at(z - side * distance, y, c)
+        return remote(rows_all.at[block], rows_all.at[block],
+                      line_send.at[distance, (side + 1) // 2, place], rows_recv.at[block], target)
+
+    def on_line(place):
+        return (place >= 0) & (place < LINE)
+
+    for side in (1, -1):
+        @pl.when(on_line(z + side))
+        def _():
+            line_copy(0, side).start()
     push_rows(me, ypart)
     push_rows(me, sib)
 
@@ -355,22 +372,30 @@
     up_first = remote(up_send.at[1 - c], up_sib, up_ssem.at[0], up_rsem.at[0], sib)
     up_first.start()
 
-    for k in range(1, LINE):
-        block = at(hop(k), y, c)
-        take_rows(block)
-        push_rows(block, ypart)
-        push_rows(block, sib)
+    for distance in range(1, LINE):
+        for side in (1, -1):
+            @pl.when(on_line(z - side * distance))
+            def _():
+                take_rows(at(z - side * distance, y, c))
+
+                @pl.when(on_line(z + side))
+                def _():
+                    line_copy(distance, side).start()
+
+                fan_copy(distance, side, ypart, 1).start()
+                fan_copy(distance, side, sib, 2).start()
 
     up_first.wait()
     up_mid[...] = up_send[c] + up_sib[...]
-    up_second = remote(up_mid.at[1 - y], up_y, up_ssem.at[1], up_rsem.at[1], ypart)
-    up_second.start()
 
     reached, cosines, sines = [], [], []
     node = lax.broadcasted_iota(jnp.int32, (tree, tree), 1)
     own = lax.broadcasted_iota(jnp.int32, (tree, tree), 0)
+    unit = jnp.where(own == node, 1.0, 0.0).astype(jnp.bfloat16)
     for r in range(requests):
-        hot = jnp.where((parents[r] == node) | (own == node), 1.0, 0.0)
+        hot = jnp.where((parents[r:r + 1] == own) | (own == node), 1.0, 0.0)
+        hot = lax.dot_general(hot.astype(jnp.bfloat16), unit, (((0,), (0,)), ((), ())),
+                              preferred_element_type=jnp.float32)
         for _ in range(tree.bit_length()):
             short = hot.astype(jnp.bfloat16)
             hot = jnp.minimum(
@@ -387,14 +412,8 @@
         take_rows(block)
         push_rows(block, sib)
 
-    up_second.wait()
-    up_low[...] = up_mid[y] + up_y[...]
-    up_third = []
-    for k in range(1, LINE):
-        copy = remote(up_low.at[hop(k)], up_z.at[k - 1], up_ssem.at[1 + k], up_rsem.at[1 + k],
-                      at(hop(k), y, c))
-        copy.start()
-        up_third.append(copy)
+    up_second = remote(up_mid.at[1 - y], up_y, up_ssem.at[1], up_rsem.at[1], ypart)
+    up_second.start()
 
     for k in range(LINE):
         for yy in (y, 1 - y):
@@ -432,6 +451,15 @@
     low_send[0] = low.astype(jnp.bfloat16)
     first = remote(low_send.at[0], low_recv.at[0], low_ssem.at[0], low_rsem.at[0], sib)
     first.start()
+
+    up_second.wait()
+    up_low[...] = up_mid[y] + up_y[...]
+    up_third = []
+    for k in range(1, LINE):
+        copy = remote(up_low.at[hop(k)], up_z.at[k - 1], up_ssem.at[1 + k], up_rsem.at[1 + k],
+                      at(hop(k), y, c))
+        copy.start()
+        up_third.append(copy)
 
     loads[2].wait()
     loads[3].wait()
@@ -518,8 +546,6 @@
     q_copy.wait_send()
     remote(query_buf.at[1 - c], query_buf.at[1 - c], query_sem.at[0], query_sem.at[1],
            sib).wait_recv()
-    for copy in sent:
-        copy.wait_send()
 
     loads[4].wait()
     heads = CORES * q_heads
@@ -594,18 +620,20 @@
         return remote(z_send.at[n, hop(k)], z_recv.at[n, k - 1], z_ssem.at[n, k - 1],
                       z_rsem.at[n, k - 1], at(hop(k), y, c))
 
-    for n in range(OUT_CHUNKS):
+    def project(n):
         product = jnp.dot(attention[...], w_out[:, n * columns:(n + 1) * columns],
                           preferred_element_type=jnp.float32)
         for d in range(count):
             part[n, d % 2, d // 2 % 2, d // 4] = product[d * 8:(d + 1) * 8]
         sib_copy(n).start()
-    for n in range(OUT_CHUNKS):
+
+    def sum_pair(n):
         sib_copy(n).wait()
         away = part[n, c, 1 - y] + part_sib[n, 1 - y]
         y_send[n] = away.reshape(LINE * 8, columns).astype(jnp.bfloat16)
         y_copy(n).start()
-    for n in range(OUT_CHUNKS):
+
+    def sum_y(n):
         y_copy(n).wait()
         held = (part[n, c, y] + part_sib[n, y]) + y_recv[n].astype(jnp.float32).reshape(
             LINE, 8, columns)
@@ -615,6 +643,14 @@
                 [held[d, :, :columns // 2], held[d, :, columns // 2:]], axis=0).astype(jnp.bfloat16)
         for k in range(1, LINE):
             z_copy(n, k).start()
+
+    for turn in range(OUT_CHUNKS + 2):
+        if turn < OUT_CHUNKS:
+            project(turn)
+        if 1 <= turn <= OUT_CHUNKS:
+            sum_pair(turn - 1)
+        if turn >= 2:
+            sum_y(turn - 2)
     for n in range(OUT_CHUNKS):
         total = part_sib[n, 0, z]
         for k in range(1, LINE):
@@ -622,6 +658,20 @@
             landed = z_recv[n, k - 1].astype(jnp.float32)
             total = total + jnp.concatenate([landed[:8], landed[8:]], axis=1)
         out[:, n * columns:(n + 1) * columns] = total.astype(jnp.bfloat16)
+
+    for copy in sent:
+        copy.wait_send()
+    for distance in range(LINE):
+        for side in (1, -1):
+            @pl.when(on_line(z - side * distance) & on_line(z + side))
+            def _():
+                line_copy(distance, side).wait_send()
+
+            if distance > 0:
+                @pl.when(on_line(z - side * distance))
+                def _():
+                    fan_copy(distance, side, ypart, 1).wait_send()
+                    fan_copy(distance, side, sib, 2).wait_send()
 
 
 def fused_body(
@@ -632,8 +682,8 @@
     rows, model = layer_input.shape
     half = model // 2
     packed = layer_input.reshape(rows, 2, half).transpose(1, 0, 2).reshape(2 * rows, half)
-    exponents = jnp.arange(64, dtype=jnp.float32) * (2.0 / 128)
-    inverse = jnp.exp(exponents * -math.log(rope_base))[None]
+    exponents = np.arange(64) * (2.0 / 128)
+    inverse = jnp.asarray(np.exp(exponents * -math.log(rope_base))[None].astype(np.float32))
     bf, f32 = jnp.bfloat16, jnp.float32
     count = 16
     rank = adapter_up_weight.shape[1]
@@ -653,13 +703,12 @@
         pltpu.VMEM((3, ranks, 128), bf), pltpu.VMEM((5, ranks, 128), bf),
         pltpu.VMEM((2, 2, 4, 64, 128), bf), pltpu.VMEM((2, 2, 32, 128), bf),
         pltpu.VMEM((2, 32, 128), bf), pltpu.VMEM((2, 32, 128), bf),
-        pltpu.VMEM((8, 128), f32), pltpu.VMEM((8, 128), f32), pltpu.VMEM((8, 128), f32),
         pltpu.VMEM((2, 2, 3, 256, 128), f32), pltpu.VMEM((2, 3, 256, 128), f32),
         pltpu.VMEM((128, 512), bf),
         pltpu.VMEM((n, 2, 2, 4, 8, columns), f32), pltpu.VMEM((n, 2, 4, 8, columns), f32),
         pltpu.VMEM((n, 32, columns), bf), pltpu.VMEM((n, 32, columns), bf),
         pltpu.VMEM((n, 4, 16, columns // 2), bf), pltpu.VMEM((n, 3, 16, columns // 2), bf),
-        dma((6,)), dma((15,)), dma((count,)), dma((5,)), dma((5,)), dma((5,)), dma((5,)),
+        dma((6,)), dma((6,)), dma((4, 2, 3)), dma((count,)), dma((5,)), dma((5,)), dma((5,)), dma((5,)),
         dma((2,)), dma((2,)), dma((2,)), dma((2,)), dma((2,)),
         dma((n,)), dma((n,)), dma((n,)), dma((n,)), dma((n, 3)), dma((n, 3)),
     ]
@@ -678,7 +727,7 @@
             flops=5 * 10**9, bytes_accessed=25 * 2**20, transcendentals=4 * 2**20),
         name="fused_layer",
     )(adapter_storage_index, request_adapter, cached_length, packed, input_norm_gain[None],
-      parent_node[:, :, None], inverse, adapter_down_weight, adapter_up_weight,
+      parent_node, inverse, adapter_down_weight, adapter_up_weight,
       query_weight, key_value_weight, output_weight, cached_key_value)
 
 

time: 81.9 us -> 73.9 us (0.902)
  Pallas kernels: 78.2 us -> 72.2 us
  local copies, waits for them, and re-layouts: 2.98 us -> 1.57 us
    pallas_call x1, Pallas kernels: 78.2 us -> 72.2 us  [fused_body(): pl.pallas_call(fused_kernel, out_shape=jax.ShapeDtypeStruct((rows, model)...]
    broadcast_in_dim x1 -> x0, local copies, waits for them, and re-layouts: 1.41 us -> none  [fused_body(): parent_node[:, :, None]]
where the time goes in v2:
time: 73.9 us; the launch traced here: 73.8 us
  Pallas kernels  72.2 us (98%)
  local copies, waits for them, and re-layouts  1.57 us (2%)
    pallas_call x1, Pallas kernels, fused_body(): pl.pallas_call(fused_kernel, out_shape=jax.ShapeDtypeStruct((rows, model)...  72.2 us
    unnamed x1, local copies, waits for them, and re-layouts  1.57 us

profile of v2, /device:TPU:0, one launch (start us, length us, event | category | flops | bytes accessed | tf_op | source)
XLA Modules:
  0.0 73.8 jit_solution(10554916932179803787)
XLA Ops:
  0.0 72.2 %fused_layer.1 = bf16[8,8192]{1,0:T(8,128)(2,1)} custom-call(s32[32]{0:T(128)} %slot_of.1, s32[2]{0:T(128)} %adapter_of.1, s32[2]{0:T(128)} %length_of.1, bf16[16,4096]{1,0:T(8,128)(2,1)} %bitcast.6, f32[1,8192]{1,0:T(1,128)} %bitcast.7, s32[2,64]{1,0:T(2,128)} %parents.1, f32[1,64]{1,0:T(1,128)} %constant.2.clone.inverse, bf16[2,48,8192]{2,1,0:T(8,128)(2,1)} %down.1, ...), custom_call_target="tpu_custom_call" | custom-call | flops 5000000000 | bytes 26214400 | tf_op jit(solution)/shard_map/fused_layer/pallas_call | solution.py:718
  72.2 1.6 %copy.15 = bf16[8,8192]{1,0:T(8,128)(2,1)} copy(bf16[8,8192]{1,0:T(8,128)(2,1)} %fused_layer.1) | data formatting | bytes 262144

commit v3 on v2

--- a/solution.py
+++ b/solution.py
@@ -407,21 +407,9 @@
         cosines.append(jnp.cos(angles))
         sines.append(jnp.sin(angles))
 
-    for k in range(LINE):
-        block = at(hop(k), 1 - y, c)
-        take_rows(block)
-        push_rows(block, sib)
-
-    up_second = remote(up_mid.at[1 - y], up_y, up_ssem.at[1], up_rsem.at[1], ypart)
-    up_second.start()
-
-    for k in range(LINE):
-        for yy in (y, 1 - y):
-            take_rows(at(hop(k), yy, 1 - c))
-
     half = rows_all.shape[2]
 
-    def norm_step(k, carry):
+    def norm_chip(k):
         parts = []
         for j in range(2):
             block = rows_all[2 * k + j].astype(jnp.float32)
@@ -433,9 +421,20 @@
             cols = slice(h * half, (h + 1) * half)
             normed[pl.ds(pl.multiple_of(k * 16, 16), 16), cols] = (
                 both * gain[:, cols]).astype(jnp.bfloat16)
-        return carry
-
-    lax.fori_loop(0, count // 2, norm_step, 0)
+
+    for k in range(LINE):
+        block = at(hop(k), 1 - y, c)
+        take_rows(block)
+        push_rows(block, sib)
+        take_rows(at(hop(k), y, 1 - c))
+        norm_chip(hop(k) * PAIR + y)
+
+    up_second = remote(up_mid.at[1 - y], up_y, up_ssem.at[1], up_rsem.at[1], ypart)
+    up_second.start()
+
+    for k in range(LINE):
+        take_rows(at(hop(k), 1 - y, 1 - c))
+        norm_chip(hop(k) * PAIR + 1 - y)
 
     nt = (((1,), (1,)), ((), ()))
     tn = (((0,), (0,)), ((), ()))

time: 73.9 us -> 73.2 us (level)
  no operation moved by 1% of the time
where the time goes in v3:
time: 73.2 us; the launch traced here: 73 us
  Pallas kernels  71.5 us (98%)
  local copies, waits for them, and re-layouts  1.57 us (2%)
    pallas_call x1, Pallas kernels, fused_body(): pl.pallas_call(fused_kernel, out_shape=jax.ShapeDtypeStruct((rows, model)...  71.5 us
    unnamed x1, local copies, waits for them, and re-layouts  1.57 us

profile of v3, /device:TPU:0, one launch (start us, length us, event | category | flops | bytes accessed | tf_op | source)
XLA Modules:
  0.0 73.0 jit_solution(16314983722270805960)
XLA Ops:
  0.0 71.5 %fused_layer.1 = bf16[8,8192]{1,0:T(8,128)(2,1)} custom-call(s32[32]{0:T(128)} %slot_of.1, s32[2]{0:T(128)} %adapter_of.1, s32[2]{0:T(128)} %length_of.1, bf16[16,4096]{1,0:T(8,128)(2,1)} %bitcast.6, f32[1,8192]{1,0:T(1,128)} %bitcast.7, s32[2,64]{1,0:T(2,128)} %parents.1, f32[1,64]{1,0:T(1,128)} %constant.2.clone.inverse, bf16[2,48,8192]{2,1,0:T(8,128)(2,1)} %down.1, ...), custom_call_target="tpu_custom_call" | custom-call | flops 5000000000 | bytes 26214400 | tf_op jit(solution)/shard_map/fused_layer/pallas_call | solution.py:717
  71.5 1.6 %copy.15 = bf16[8,8192]{1,0:T(8,128)(2,1)} copy(bf16[8,8192]{1,0:T(8,128)(2,1)} %fused_layer.1) | data formatting | bytes 262144

commit v4 on v3

--- a/solution.py
+++ b/solution.py
@@ -270,7 +270,7 @@
 MESH = pl.DeviceIdType.MESH
 LINE, PAIR, CORES = 4, 2, 2
 OUT_CHUNKS = 4
-KEY_CHUNK = 1024
+KEY_CHUNK = 2048
 lowest = -1e29
 
 

time: 73.2 us -> 72.6 us (level)
  no operation moved by 1% of the time
where the time goes in v4:
time: 72.6 us; the launch traced here: 72.4 us
  Pallas kernels  70.9 us (98%)
  local copies, waits for them, and re-layouts  1.57 us (2%)
    pallas_call x1, Pallas kernels, fused_body(): pl.pallas_call(fused_kernel, out_shape=jax.ShapeDtypeStruct((rows, model)...  70.9 us
    unnamed x1, local copies, waits for them, and re-layouts  1.57 us

profile of v4, /device:TPU:0, one launch (start us, length us, event | category | flops | bytes accessed | tf_op | source)
XLA Modules:
  0.0 72.4 jit_solution(3166643037948013575)
XLA Ops:
  0.0 70.9 %fused_layer.1 = bf16[8,8192]{1,0:T(8,128)(2,1)} custom-call(s32[32]{0:T(128)} %slot_of.1, s32[2]{0:T(128)} %adapter_of.1, s32[2]{0:T(128)} %length_of.1, bf16[16,4096]{1,0:T(8,128)(2,1)} %bitcast.6, f32[1,8192]{1,0:T(1,128)} %bitcast.7, s32[2,64]{1,0:T(2,128)} %parents.1, f32[1,64]{1,0:T(1,128)} %constant.2.clone.inverse, bf16[2,48,8192]{2,1,0:T(8,128)(2,1)} %down.1, ...), custom_call_target="tpu_custom_call" | custom-call | flops 5000000000 | bytes 26214400 | tf_op jit(solution)/shard_map/fused_layer/pallas_call | solution.py:717
  70.9 1.6 %copy.15 = bf16[8,8192]{1,0:T(8,128)(2,1)} copy(bf16[8,8192]{1,0:T(8,128)(2,1)} %fused_layer.1) | data formatting | bytes 262144
